TPU v7x, 512 devices: a whole 4x4x16 slice. The times are simulated.
512 devices in a mesh: leaf: 32 (over x, y, core), front: 16 (over z).
Axes of the slice: x: 4, y: 4, z: 16, core: 2. Of those that a mesh axis runs over, the one named last changes fastest.
Arguments:
- panel_0: float32 [2, 1024, 1024], P(None, 'front', 'leaf'), as said below
- panel_1: float32 [2, 1024, 2048], P(None, 'front', 'leaf'), as said below
- panel_2: float32 [2, 1024, 4096], P(None, 'front', 'leaf'), as said below
- panel_3: float32 [2, 1024, 8192], P(None, 'front', 'leaf'), as said below
- load_0: float32 [1024, 128], P('leaf'), may hold values from -6 to 6
- load_1: float32 [2048, 128], P('leaf'), may hold values from -6 to 6
- load_2: float32 [4096, 128], P('leaf'), may hold values from -6 to 6
- load_3: float32 [8192, 128], P('leaf'), may hold values from -6 to 6
- inflow: float32 [8, 1024, 128], P(None, 'front'), may hold values from -6 to 6
- above_solution: float32 [1024, 128], replicated, may hold values from -6 to 6
- block_maps: int32 [14, 16], replicated, may hold values from 0 to 31, as said below
Outputs:
- solution_0: float32 [1024, 128], P(('leaf', 'front'))
- solution_1: float32 [2048, 128], P(('leaf', 'front'))
- solution_2: float32 [4096, 128], P(('leaf', 'front'))
- solution_3: float32 [8192, 128], P(('leaf', 'front'))
- top_update: float32 [1024, 128], P('front')
Inputs may be any that keep to these rules, and one draw needn't show every extreme that they name: `block_maps`: the 16 entries of each row are distinct. `panel_0`: within each front the pivot block K is lower triangular with diagonal entries of 0.8 to 1.25. `panel_1`: within each front the pivot block K is lower triangular with diagonal entries of 0.8 to 1.25. `panel_2`: within each front the pivot block K is lower triangular with diagonal entries of 0.8 to 1.25. `panel_3`: within each front the pivot block K is lower triangular with diagonal entries of 0.8 to 1.25.
All inputs are finite; a program needn't handle non-finite values.
Results may differ from a plain program's by a relative error of at most 0.00013.
Values sent between devices are 32-bit elements; how exact they have to be, the bound alone decides.
No kernel may reach another device: no remote copies, remote signals or barrier semaphores. Data moves between devices by JAX's collectives and lax.ppermute only.
A program may use at most 64 MiB of HBM per device.

v0:
```python
import jax
import jax.numpy as jnp
from jax import lax
from jax.sharding import PartitionSpec as P

exact_precision = lax.Precision.HIGHEST


def partner_2(value, axis, distance):
    mask = 2**distance
    pairs = [(source, source ^ mask) for source in range(lax.axis_size(axis))]
    return lax.ppermute(value, axis, pairs)


def group_total(partial_sum, group_bits, level_id):
    leaf_pos = lax.axis_index("leaf")
    group_count = 1 << level_id
    slot_id = leaf_pos >> group_bits
    chosen = (jnp.arange(group_count, dtype=jnp.int32) == slot_id).astype(jnp.float32)
    spread_out = chosen.reshape((group_count,) + (1,) * partial_sum.ndim) * partial_sum[None]
    totals = lax.psum(spread_out, "leaf")
    return lax.dynamic_index_in_dim(totals, slot_id, 0, keepdims=False)


def group_concat(column_block, group_bits):
    leaf_pos = lax.axis_index("leaf")
    for section_bit in range(group_bits):
        partner = partner_2(column_block, "leaf", section_bit)
        upper_half = leaf_pos >> section_bit & 1 == 1
        column_block = jnp.where(
            upper_half,
            jnp.concatenate([partner, column_block], 0),
            jnp.concatenate([column_block, partner], 0),
        )
    return column_block


def place_blocks(map_row, values, block_rows):
    block_count = map_row.shape[0]
    targets = jnp.arange(2 * block_count, dtype=jnp.int32)
    selector_matrix = (targets[:, None] == map_row[None, :]).astype(jnp.float32)
    factor_blocks = values.reshape(block_count, block_rows, values.shape[1])
    return jnp.einsum("du,uye->dye", selector_matrix, factor_blocks, precision=exact_precision)


def lift_update(update_block, level_id, group_bits, block_maps, sep_rows):
    leaf_pos = lax.axis_index("leaf")
    front_pos = lax.axis_index("front")
    block_rows = update_block.shape[0]
    block_count = sep_rows // block_rows
    group_size = 1 << group_bits
    child_id = leaf_pos >> group_bits
    base_row = (1 << level_id) - 2
    own_map = lax.dynamic_index_in_dim(block_maps, base_row + child_id, 0, keepdims=False)
    parent_pos = leaf_pos % (2 * group_size)
    parent_rows = sep_rows // (2 * group_size)
    other_map = lax.dynamic_index_in_dim(block_maps, base_row + (child_id ^ 1), 0, keepdims=False)
    partner_block = partner_2(update_block, "leaf", group_bits)
    own_full, other_full = (
        lax.all_gather(update_block, "front", axis=0, tiled=True),
        lax.all_gather(partner_block, "front", axis=0, tiled=True),
    )
    placed = place_blocks(own_map, own_full, block_rows) + place_blocks(
        other_map, other_full, block_rows
    )
    separator = placed[:block_count].reshape(sep_rows, -1)
    sep_part = lax.dynamic_slice_in_dim(separator, parent_pos * parent_rows, parent_rows, 0)
    border = lax.dynamic_index_in_dim(placed, block_count + front_pos, 0, keepdims=False)
    return (sep_part, border)


def on_device(
    panel_0,
    panel_1,
    panel_2,
    panel_3,
    load_0,
    load_1,
    load_2,
    load_3,
    inflow,
    above_solution,
    block_maps,
):
    panels = (panel_0, panel_1, panel_2, panel_3)
    load_list = (load_0, load_1, load_2, load_3)
    level_count = len(panels)
    leaf_pos = lax.axis_index("leaf")
    front_pos = lax.axis_index("front")
    front_count = lax.axis_size("front")
    total_bits = lax.axis_size("leaf").bit_length() - 1
    block_rows = panel_0.shape[1]
    sep_rows = block_rows * front_count
    solved = [None] * level_count
    lifted = None
    top_block = None
    for level_id in range(level_count - 1, -1, -1):
        group_bits = total_bits - level_id
        right_side = load_list[level_id]
        if level_id == level_count - 1:
            front_id = leaf_pos >> group_bits
            border = lax.dynamic_index_in_dim(inflow, front_id, 0, keepdims=False)
        else:
            right_side = right_side + lifted[0]
            border = lifted[1]
        partial_sum = jnp.einsum(
            "ksc,cr->ksr", panels[level_id], right_side, precision=exact_precision
        )
        totals = group_total(partial_sum, group_bits, level_id)
        solved[level_id] = totals[0]
        update_block = border - totals[1]
        if level_id > 0:
            lifted = lift_update(update_block, level_id, group_bits, block_maps, sep_rows)
        else:
            top_block = update_block
    upper_full = above_solution
    upper_block = lax.dynamic_slice_in_dim(above_solution, front_pos * block_rows, block_rows, 0)
    targets = jnp.arange(2 * front_count, dtype=jnp.int32)
    pieces = []
    for level_id in range(level_count):
        group_bits = total_bits - level_id
        stacked = jnp.stack([solved[level_id], -upper_block])
        partial_sum = jnp.einsum(
            "ksc,ksr->cr", panels[level_id], stacked, precision=exact_precision
        )
        column_block = lax.psum(partial_sum, "front")
        span_rows = column_block.shape[0] // front_count
        pieces.append(lax.dynamic_slice_in_dim(column_block, front_pos * span_rows, span_rows, 0))
        if level_id < level_count - 1:
            full_solution = group_concat(column_block, group_bits)
            ancestor_blocks = jnp.concatenate([full_solution, upper_full], 0).reshape(
                2 * front_count, block_rows, -1
            )
            child_id = leaf_pos >> group_bits - 1
            child_map = lax.dynamic_index_in_dim(
                block_maps, (2 << level_id) - 2 + child_id, 0, keepdims=False
            )
            selector_matrix = (child_map[:, None] == targets[None, :]).astype(jnp.float32)
            upper_factor_blocks = jnp.einsum(
                "gq,qzk->gzk", selector_matrix, ancestor_blocks, precision=exact_precision
            )
            upper_full = upper_factor_blocks.reshape(sep_rows, -1)
            upper_block = lax.dynamic_index_in_dim(
                upper_factor_blocks, front_pos, 0, keepdims=False
            )
    return (pieces[0], pieces[1], pieces[2], pieces[3], top_block)


def solution(mesh):
    in_specs = (
        P(None, "front", "leaf"),
        P(None, "front", "leaf"),
        P(None, "front", "leaf"),
        P(None, "front", "leaf"),
        P("leaf", None),
        P("leaf", None),
        P("leaf", None),
        P("leaf", None),
        P(None, "front", None),
        P(),
        P(),
    )
    out_specs = (
        P(("leaf", "front"), None),
        P(("leaf", "front"), None),
        P(("leaf", "front"), None),
        P(("leaf", "front"), None),
        P("front", None),
    )
    return jax.shard_map(
        on_device, mesh=mesh, in_specs=in_specs, out_specs=out_specs, check_vma=False
    )
```

profile of v0, /device:TPU:2, one launch (start us, length us, event | category | flops | bytes accessed | tf_op | source)
XLA Modules:
  0.0 1208.8 jit_solution(1407500976551751530)
XLA Ops:
  8.1 1.2 fusion.16
  11.1 138.3 %all-reduce.7.cloned.1.call-done = f32[8,2,64,128]{3,2,1,0:T(8,128)} async-done(((f32[8,2,64,128]{3,2,1,0:T(8,128)}), f32[8,2,64,128]{3,2,1,0:T(8,128)}) %all-reduce.7.cloned.1.call-update) | async-done | bytes 524304 | tf_op jit(solution)/shard_map/psum | solution.py:21
  150.2 4.2 collective-permute-start
  154.4 33.1 %all_gather.18 = f32[1024,128]{1,0:T(8,128)S(1)} all-gather(f32[64,128]{1,0:T(8,128)S(1)} %fusion.32), channel_id=1, replica_groups=mesh['leaf'=32,'front'=16] {'front'}, dimensions={0}, use_global_device_ids=true | all-gather | bytes 557056 | tf_op jit(solution)/shard_map/all_gather | solution.py:60
  188.5 30.6 %all_gather.19 = f32[1024,128]{1,0:T(8,128)S(1)} all-gather(f32[64,128]{1,0:T(8,128)S(1)} %collective-permute-done), channel_id=1, replica_groups=mesh['leaf'=32,'front'=16] {'front'}, dimensions={0}, use_global_device_ids=true | all-gather | bytes 557056 | tf_op jit(solution)/shard_map/all_gather | solution.py:61
  219.1 1.0 convolution_add_fusion.2
  222.2 127.9 %all-reduce.9.cloned.1.call-done = f32[4,2,64,128]{3,2,1,0:T(8,128)} async-done(((f32[4,2,64,128]{3,2,1,0:T(8,128)}), f32[4,2,64,128]{3,2,1,0:T(8,128)}) %all-reduce.9.cloned.1.call-update) | async-done | bytes 262160 | tf_op jit(solution)/shard_map/psum | solution.py:21
  350.8 3.0 collective-permute-start.1
  353.8 33.6 %all_gather.20 = f32[1024,128]{1,0:T(8,128)S(1)} all-gather(f32[64,128]{1,0:T(8,128)S(1)} %fusion.31), channel_id=1, replica_groups=mesh['leaf'=32,'front'=16] {'front'}, dimensions={0}, use_global_device_ids=true | all-gather | bytes 557056 | tf_op jit(solution)/shard_map/all_gather | solution.py:60
  388.3 30.1 %all_gather.21 = f32[1024,128]{1,0:T(8,128)S(1)} all-gather(f32[64,128]{1,0:T(8,128)S(1)} %collective-permute-done.1), channel_id=1, replica_groups=mesh['leaf'=32,'front'=16] {'front'}, dimensions={0}, use_global_device_ids=true | all-gather | bytes 557056 | tf_op jit(solution)/shard_map/all_gather | solution.py:61
  421.3 126.1 %all-reduce.11.cloned.1.call-done = f32[2,2,64,128]{3,2,1,0:T(8,128)} async-done(((f32[2,2,64,128]{3,2,1,0:T(8,128)}), f32[2,2,64,128]{3,2,1,0:T(8,128)}) %all-reduce.11.cloned.1.call-update) | async-done | bytes 131088 | tf_op jit(solution)/shard_map/psum | solution.py:21
  548.2 5.2 collective-permute-start.2
  553.4 33.3 %all_gather.22 = f32[1024,128]{1,0:T(8,128)S(1)} all-gather(f32[64,128]{1,0:T(8,128)S(1)} %fusion.30), channel_id=1, replica_groups=mesh['leaf'=32,'front'=16] {'front'}, dimensions={0}, use_global_device_ids=true | all-gather | bytes 557056 | tf_op jit(solution)/shard_map/all_gather | solution.py:60
  587.6 30.3 %all_gather.23 = f32[1024,128]{1,0:T(8,128)S(1)} all-gather(f32[64,128]{1,0:T(8,128)S(1)} %collective-permute-done.2), channel_id=1, replica_groups=mesh['leaf'=32,'front'=16] {'front'}, dimensions={0}, use_global_device_ids=true | all-gather | bytes 557056 | tf_op jit(solution)/shard_map/all_gather | solution.py:61
  617.9 1.0 convolution_add_fusion
  620.7 120.9 %all-reduce.13.cloned.1.call-done = f32[1,2,64,128]{3,2,1,0:T(8,128)} async-done(((f32[1,2,64,128]{3,2,1,0:T(8,128)}), f32[1,2,64,128]{3,2,1,0:T(8,128)}) %all-reduce.13.cloned.1.call-update) | async-done | bytes 65552 | tf_op jit(solution)/shard_map/psum | solution.py:21
  742.6 56.8 %psum.60 = f32[32,128]{1,0:T(8,128)S(1)} all-reduce(f32[32,128]{1,0:T(8,128)S(1)} %convolution_bitcast_fusion.5), channel_id=1, replica_groups=mesh['leaf'=32,'front'=16] {'front'}, use_global_device_ids=true, to_apply=%region_4.5 | all-reduce | flops 4096 | bytes 32768 | tf_op jit(solution)/shard_map/psum | solution.py:126
  799.4 1.9 collective-permute-start.3
  801.3 1.1 collective-permute-done.3
  802.4 3.4 collective-permute-start.4
  805.8 2.4 collective-permute-done.4
  808.2 4.6 collective-permute-start.5
  812.8 3.1 collective-permute-done.5
  815.9 3.3 collective-permute-start.6
  819.3 3.5 collective-permute-done.6
  822.8 4.1 collective-permute-start.7
  827.6 4.9 collective-permute-done.7
  832.7 1.1 fusion.5
  834.2 53.5 %psum.61 = f32[64,128]{1,0:T(8,128)S(1)} all-reduce(f32[64,128]{1,0:T(8,128)S(1)} %convolution_bitcast_fusion.4), channel_id=1, replica_groups=mesh['leaf'=32,'front'=16] {'front'}, use_global_device_ids=true, to_apply=%region_5.6 | all-reduce | flops 8192 | bytes 65536 | tf_op jit(solution)/shard_map/psum | solution.py:126
  887.7 1.9 collective-permute-start.8
  889.6 1.2 collective-permute-done.8
  890.8 3.4 collective-permute-start.9
  894.1 2.8 collective-permute-done.9
  896.9 4.6 collective-permute-start.10
  901.5 3.8 collective-permute-done.10
  905.3 3.5 collective-permute-start.11
  909.8 3.8 collective-permute-done.11
  913.7 1.1 fusion.3
  915.9 129.0 %all-reduce.15.cloned.1.call-done = f32[128,128]{0,1:T(8,128)} async-done(((f32[128,128]{0,1:T(8,128)}), f32[128,128]{0,1:T(8,128)}) %all-reduce.15.cloned.1.call-update) | async-done | bytes 65552 | tf_op jit(solution)/shard_map/psum | solution.py:126
  1044.9 1.9 collective-permute-start.12
  1046.8 1.4 collective-permute-done.12
  1049.1 3.4 collective-permute-start.13
  1053.4 3.2 collective-permute-done.13
  1056.6 4.9 collective-permute-start.14
  1063.1 4.4 collective-permute-done.14
  1068.0 1.1 fusion.1
  1069.2 1.0 convolution_bitcast_fusion
  1071.7 128.7 %all-reduce.17.cloned.1.call-done = f32[256,128]{0,1:T(8,128)} async-done(((f32[256,128]{0,1:T(8,128)}), f32[256,128]{0,1:T(8,128)}) %all-reduce.17.cloned.1.call-update) | async-done | bytes 131088 | tf_op jit(solution)/shard_map/psum | solution.py:126
  (101 shorter events, 25.7 us)
Async XLA Ops:
  7.2 0.9 copy-start
  7.2 142.3 %all-reduce.7.cloned.1.call-start = ((), (), s32[]{:S(2)}) async-start(), calls=%async_computation | async-start | bytes 1048576 | tf_op jit(solution)/shard_map/psum | solution.py:21
  10.2 339.9 %all-reduce.9.cloned.1.call-start = ((), (), s32[]{:S(2)}) async-start(), calls=%async_computation.1 | async-start | bytes 524288 | tf_op jit(solution)/shard_map/psum | solution.py:21
  150.2 38.2 %collective-permute-start = (f32[64,128]{1,0:T(8,128)S(1)}, f32[64,128]{1,0:T(8,128)S(1)}, u32[]{:S(2)}, u32[]{:S(2)}) collective-permute-start(f32[64,128]{1,0:T(8,128)S(1)} %fusion.32), channel_id=1, source_target_pairs={{0,64},{16,80},{32,96},{48,112},{64,0},{80,16},{96,32},{112,48},{1... | collective-permute-start | bytes 98312 | tf_op jit(solution)/shard_map/ppermute | solution.py:12
  220.1 0.8 copy-start.3
  220.1 0.9 copy-start.7
  222.0 325.4 %all-reduce.11.cloned.1.call-start = ((), (), s32[]{:S(2)}) async-start(), calls=%async_computation.2 | async-start | bytes 262144 | tf_op jit(solution)/shard_map/psum | solution.py:21
  350.8 37.5 %collective-permute-start.1 = (f32[64,128]{1,0:T(8,128)S(1)}, f32[64,128]{1,0:T(8,128)S(1)}, u32[]{:S(2)}, u32[]{:S(2)}) collective-permute-start(f32[64,128]{1,0:T(8,128)S(1)} %fusion.31), channel_id=1, source_target_pairs={{0,128},{16,144},{32,160},{48,176},{64,192},{80,208},{96,224},{112... | collective-permute-start | bytes 98312 | tf_op jit(solution)/shard_map/ppermute | solution.py:12
  419.4 0.8 copy-start.2
  419.5 0.8 copy-start.8
  421.2 320.4 %all-reduce.13.cloned.1.call-start = ((), (), s32[]{:S(2)}) async-start(), calls=%async_computation.3 | async-start | bytes 131072 | tf_op jit(solution)/shard_map/psum | solution.py:21
  548.2 39.5 %collective-permute-start.2 = (f32[64,128]{1,0:T(8,128)S(1)}, f32[64,128]{1,0:T(8,128)S(1)}, u32[]{:S(2)}, u32[]{:S(2)}) collective-permute-start(f32[64,128]{1,0:T(8,128)S(1)} %fusion.30), channel_id=1, source_target_pairs={{0,256},{16,272},{32,288},{48,304},{64,320},{80,336},{96,352},{112... | collective-permute-start | bytes 98312 | tf_op jit(solution)/shard_map/ppermute | solution.py:12
  618.9 0.8 copy-start.5
  619.0 0.8 copy-start.9
  619.0 1.7 copy-start.1
  620.7 424.2 %all-reduce.15.cloned.1.call-start = ((), (), s32[]{:S(2)}) async-start(), calls=%async_computation.4 | async-start | bytes 131072 | tf_op jit(solution)/shard_map/psum | solution.py:126
  799.4 3.1 collective-permute-start.3
  802.4 5.8 collective-permute-start.4
  808.2 7.7 collective-permute-start.5
  815.9 6.9 collective-permute-start.6
  822.8 9.8 collective-permute-start.7
  887.7 3.1 collective-permute-start.8
  890.8 6.2 collective-permute-start.9
  896.9 8.4 collective-permute-start.10
  905.3 8.3 collective-permute-start.11
  915.9 284.5 %all-reduce.17.cloned.1.call-start = ((), (), s32[]{:S(2)}) async-start(), calls=%async_computation.5 | async-start | bytes 262144 | tf_op jit(solution)/shard_map/psum | solution.py:126
  1044.9 3.3 collective-permute-start.12
  1049.1 7.5 collective-permute-start.13
  1053.4 8.8 copy-start.6
  1056.6 10.9 collective-permute-start.14
  1070.1 0.8 copy-start.4
Sparse Core Ops, SparseCore 0:
  11.2 138.1 all-reduce.6
  222.1 127.8 all-reduce.8
  421.4 126.0 all-reduce.10
  620.8 120.7 all-reduce.12
  916.0 128.8 all-reduce.14
  1070.3 130.0 all-reduce.16
where the time goes:
time: 1210 us
  waiting for transfers between devices  806 us (67%)
  blocking collectives  301 us (25%)
  starting transfers between devices  53.6 us (4%)
  between operations  14.8 us (1%)
  matrix products  13.7 us (1%)
    psum x4, waiting for transfers between devices, group_total(): totals = lax.psum(spread_out, 'leaf')  513 us
    psum x2, waiting for transfers between devices, on_device(): column_block = lax.psum(partial_sum, 'front')  258 us
    psum x2, blocking collectives, on_device(): column_block = lax.psum(partial_sum, 'front')  110 us
    all_gather x3, blocking collectives, lift_update(): lax.all_gather(update_block, 'front', axis=0, tiled=True)  100 us
    all_gather x3, blocking collectives, lift_update(): lax.all_gather(partner_block, 'front', axis=0, tiled=True)  91 us
    ppermute x15, starting transfers between devices, partner_2(): return lax.ppermute(value, axis, pairs)  53.4 us
    ppermute x15, waiting for transfers between devices, partner_2(): return lax.ppermute(value, axis, pairs)  35.6 us
  transfers between devices with their start and end apart: 21, of which 18 were waited for; matrix products, arithmetic and copies ran while one was open for 1% of the time, Pallas kernels for 0%

commit v1 on v0

--- a/solution.py
+++ b/solution.py
@@ -18,7 +18,9 @@
     slot_id = leaf_pos >> group_bits
     chosen = (jnp.arange(group_count, dtype=jnp.int32) == slot_id).astype(jnp.float32)
     spread_out = chosen.reshape((group_count,) + (1,) * partial_sum.ndim) * partial_sum[None]
-    totals = lax.psum(spread_out, "leaf")
+    totals = spread_out
+    for hop in (1, 2, 4, 8, 16):
+        totals = totals + lax.ppermute(totals, "leaf", [(dev, dev ^ hop) for dev in range(32)])
     return lax.dynamic_index_in_dim(totals, slot_id, 0, keepdims=False)
 
 

time: 1210 us -> 856 us (0.71)
  waiting for transfers between devices: 806 us -> 408 us
  starting transfers between devices: 53.6 us -> 112 us
    psum x4 -> x0, waiting for transfers between devices: 513 us -> none  [group_total(): totals = lax.psum(spread_out, 'leaf')]
    ppermute x0 -> x20, waiting for transfers between devices: none -> 111 us  [group_total(): lax.ppermute(totals, 'leaf', [(dev, dev ^ hop) for dev in range(32)])]
    ppermute x0 -> x20, starting transfers between devices: none -> 65 us  [group_total(): lax.ppermute(totals, 'leaf', [(dev, dev ^ hop) for dev in range(32)])]
  transfers between devices with their start and end apart: 21 -> 37, of which waited for: 18 -> 34; matrix products, arithmetic and copies ran while one was open for 1% -> 1% of each run, Pallas kernels for 0% -> 0%
where the time goes in v1:
time: 856 us; the launch traced here: 855 us
  waiting for transfers between devices  408 us (48%)
  blocking collectives  293 us (34%)
  starting transfers between devices  112 us (13%)
  between operations  15.1 us (2%)
  matrix products  13.1 us (2%)
  local copies, waits for them, and re-layouts  10.4 us (1%)
    psum x2, waiting for transfers between devices, on_device(): column_block = lax.psum(partial_sum, 'front')  255 us
    ppermute x20, waiting for transfers between devices, group_total(): lax.ppermute(totals, 'leaf', [(dev, dev ^ hop) for dev in range(32)])  111 us
    psum x2, blocking collectives, on_device(): column_block = lax.psum(partial_sum, 'front')  107 us
    all_gather x3, blocking collectives, lift_update(): lax.all_gather(update_block, 'front', axis=0, tiled=True)  99 us
    all_gather x3, blocking collectives, lift_update(): lax.all_gather(partner_block, 'front', axis=0, tiled=True)  86.3 us
    ppermute x20, starting transfers between devices, group_total(): lax.ppermute(totals, 'leaf', [(dev, dev ^ hop) for dev in range(32)])  65 us
    ppermute x15, starting transfers between devices, partner_2(): return lax.ppermute(value, axis, pairs)  46.7 us
    ppermute x15, waiting for transfers between devices, partner_2(): return lax.ppermute(value, axis, pairs)  41.7 us
  transfers between devices with their start and end apart: 37, of which 34 were waited for; matrix products, arithmetic and copies ran while one was open for 1% of the time, Pallas kernels for 0%

profile of v1, /device:TPU:2, one launch (start us, length us, event | category | flops | bytes accessed | tf_op | source)
XLA Modules:
  0.0 854.6 jit_solution(5856727346833359832)
XLA Ops:
  13.3 3.5 collective-permute-start.1
  16.8 12.4 %collective-permute-done.1 = f32[8,2,64,128]{3,2,1,0:T(8,128)S(1)} collective-permute-done((f32[8,2,64,128]{3,2,1,0:T(8,128)S(1)}, f32[8,2,64,128]{3,2,1,0:T(8,128)S(1)}, u32[]{:S(2)}, u32[]{:S(2)}) %collective-permute-start.1) | collective-permute-done | bytes 524320 | tf_op jit(solution)/shard_map/ppermute | solution.py:23
  29.3 5.1 collective-permute-start.2
  34.4 11.4 %collective-permute-done.2 = f32[8,2,64,128]{3,2,1,0:T(8,128)S(1)} collective-permute-done((f32[8,2,64,128]{3,2,1,0:T(8,128)S(1)}, f32[8,2,64,128]{3,2,1,0:T(8,128)S(1)}, u32[]{:S(2)}, u32[]{:S(2)}) %collective-permute-start.2) | collective-permute-done | bytes 524320 | tf_op jit(solution)/shard_map/ppermute | solution.py:23
  45.9 7.8 collective-permute-start.3
  53.7 10.5 %collective-permute-done.3 = f32[8,2,64,128]{3,2,1,0:T(8,128)S(1)} collective-permute-done((f32[8,2,64,128]{3,2,1,0:T(8,128)S(1)}, f32[8,2,64,128]{3,2,1,0:T(8,128)S(1)}, u32[]{:S(2)}, u32[]{:S(2)}) %collective-permute-start.3) | collective-permute-done | bytes 524320 | tf_op jit(solution)/shard_map/ppermute | solution.py:23
  67.1 12.1 %collective-permute-done.4 = f32[8,2,64,128]{3,2,1,0:T(8,128)S(1)} collective-permute-done((f32[8,2,64,128]{3,2,1,0:T(8,128)S(1)}, f32[8,2,64,128]{3,2,1,0:T(8,128)S(1)}, u32[]{:S(2)}, u32[]{:S(2)}) %collective-permute-start.4) | collective-permute-done | bytes 524320 | tf_op jit(solution)/shard_map/ppermute | solution.py:23
  82.8 36.3 %all_gather.18 = f32[1024,128]{1,0:T(8,128)S(1)} all-gather(f32[64,128]{1,0:T(8,128)S(1)} %fusion.34), channel_id=1, replica_groups=mesh['leaf'=32,'front'=16] {'front'}, dimensions={0}, use_global_device_ids=true | all-gather | bytes 557056 | tf_op jit(solution)/shard_map/all_gather | solution.py:62
  120.0 28.7 %all_gather.19 = f32[1024,128]{1,0:T(8,128)S(1)} all-gather(f32[64,128]{1,0:T(8,128)S(1)} %collective-permute-done.5), channel_id=1, replica_groups=mesh['leaf'=32,'front'=16] {'front'}, dimensions={0}, use_global_device_ids=true | all-gather | bytes 557056 | tf_op jit(solution)/shard_map/all_gather | solution.py:63
  156.9 7.8 collective-permute-done.7
  167.5 8.2 collective-permute-done.8
  178.2 6.0 collective-permute-done.9
  184.2 4.0 collective-permute-start.10
  188.4 5.6 collective-permute-done.10
  196.5 31.4 %all_gather.20 = f32[1024,128]{1,0:T(8,128)S(1)} all-gather(f32[64,128]{1,0:T(8,128)S(1)} %fusion.33), channel_id=1, replica_groups=mesh['leaf'=32,'front'=16] {'front'}, dimensions={0}, use_global_device_ids=true | all-gather | bytes 557056 | tf_op jit(solution)/shard_map/all_gather | solution.py:62
  228.8 28.7 %all_gather.21 = f32[1024,128]{1,0:T(8,128)S(1)} all-gather(f32[64,128]{1,0:T(8,128)S(1)} %collective-permute-done.11), channel_id=1, replica_groups=mesh['leaf'=32,'front'=16] {'front'}, dimensions={0}, use_global_device_ids=true | all-gather | bytes 557056 | tf_op jit(solution)/shard_map/all_gather | solution.py:63
  265.8 4.7 collective-permute-done.13
  270.6 3.9 collective-permute-start.14
  274.5 4.5 collective-permute-done.14
  279.0 3.4 collective-permute-start.15
  282.4 3.5 collective-permute-done.15
  285.8 4.3 collective-permute-start.16
  290.3 3.9 collective-permute-done.16
  294.2 4.3 collective-permute-start.17
  298.6 31.4 %all_gather.22 = f32[1024,128]{1,0:T(8,128)S(1)} all-gather(f32[64,128]{1,0:T(8,128)S(1)} %fusion.32), channel_id=1, replica_groups=mesh['leaf'=32,'front'=16] {'front'}, dimensions={0}, use_global_device_ids=true | all-gather | bytes 557056 | tf_op jit(solution)/shard_map/all_gather | solution.py:62
  330.9 28.9 %all_gather.23 = f32[1024,128]{1,0:T(8,128)S(1)} all-gather(f32[64,128]{1,0:T(8,128)S(1)} %collective-permute-done.17), channel_id=1, replica_groups=mesh['leaf'=32,'front'=16] {'front'}, dimensions={0}, use_global_device_ids=true | all-gather | bytes 557056 | tf_op jit(solution)/shard_map/all_gather | solution.py:63
  367.4 3.7 collective-permute-done.19
  371.2 3.9 collective-permute-start.20
  375.0 3.8 collective-permute-done.20
  378.8 3.7 collective-permute-start.21
  388.0 4.6 collective-permute-done.22
  392.9 54.6 %psum.28 = f32[32,128]{1,0:T(8,128)S(1)} all-reduce(f32[32,128]{1,0:T(8,128)S(1)} %convolution_bitcast_fusion.5), channel_id=1, replica_groups=mesh['leaf'=32,'front'=16] {'front'}, use_global_device_ids=true, to_apply=%region_0.1 | all-reduce | flops 4096 | bytes 32768 | tf_op jit(solution)/shard_map/psum | solution.py:128
  456.4 3.6 collective-permute-start.25
  460.0 4.0 collective-permute-done.25
  464.0 3.9 collective-permute-start.26
  474.0 6.7 collective-permute-done.27
  483.0 52.7 %psum.29 = f32[64,128]{1,0:T(8,128)S(1)} all-reduce(f32[64,128]{1,0:T(8,128)S(1)} %convolution_bitcast_fusion.4), channel_id=1, replica_groups=mesh['leaf'=32,'front'=16] {'front'}, use_global_device_ids=true, to_apply=%region_1.2 | all-reduce | flops 8192 | bytes 65536 | tf_op jit(solution)/shard_map/psum | solution.py:128
  541.3 3.7 collective-permute-done.29
  544.9 3.6 collective-permute-start.30
  548.6 4.7 collective-permute-done.30
  553.3 3.9 collective-permute-start.31
  557.5 4.1 collective-permute-done.31
  564.6 126.0 %all-reduce.3.cloned.1.call-done = f32[128,128]{0,1:T(8,128)} async-done(((f32[128,128]{0,1:T(8,128)}), f32[128,128]{0,1:T(8,128)}) %all-reduce.3.cloned.1.call-update) | async-done | bytes 65552 | tf_op jit(solution)/shard_map/psum | solution.py:128
  694.9 3.4 collective-permute-start.33
  698.4 4.0 collective-permute-done.33
  702.4 4.9 collective-permute-start.34
  708.9 4.4 collective-permute-done.34
  717.5 128.7 %all-reduce.5.cloned.1.call-done = f32[256,128]{0,1:T(8,128)} async-done(((f32[256,128]{0,1:T(8,128)}), f32[256,128]{0,1:T(8,128)}) %all-reduce.5.cloned.1.call-update) | async-done | bytes 131088 | tf_op jit(solution)/shard_map/psum | solution.py:128
  (153 shorter events, 90.5 us)
Async XLA Ops:
  7.2 0.9 copy-start
  7.2 683.5 %all-reduce.3.cloned.1.call-start = ((), (), s32[]{:S(2)}) async-start(), calls=%async_computation | async-start | bytes 131072 | tf_op jit(solution)/shard_map/psum | solution.py:128
  9.4 3.8 collective-permute-start
  13.3 15.9 %collective-permute-start.1 = (f32[8,2,64,128]{3,2,1,0:T(8,128)S(1)}, f32[8,2,64,128]{3,2,1,0:T(8,128)S(1)}, u32[]{:S(2)}, u32[]{:S(2)}) collective-permute-start(f32[8,2,64,128]{3,2,1,0:T(8,128)S(1)} %fusion.16), channel_id=1, source_target_pairs={{0,32},{16,48},{32,0},{48,16},{64,96},{80,112},{96,64},{112,80},{1... | collective-permute-start | bytes 1572872 | tf_op jit(solution)/shard_map/ppermute | solution.py:23
  29.3 16.5 %collective-permute-start.2 = (f32[8,2,64,128]{3,2,1,0:T(8,128)S(1)}, f32[8,2,64,128]{3,2,1,0:T(8,128)S(1)}, u32[]{:S(2)}, u32[]{:S(2)}) collective-permute-start(f32[8,2,64,128]{3,2,1,0:T(8,128)S(1)} %fusion.90), channel_id=1, source_target_pairs={{0,64},{16,80},{32,96},{48,112},{64,0},{80,16},{96,32},{112,48},{1... | collective-permute-start | bytes 1572872 | tf_op jit(solution)/shard_map/ppermute | solution.py:23
  45.9 18.3 %collective-permute-start.3 = (f32[8,2,64,128]{3,2,1,0:T(8,128)S(1)}, f32[8,2,64,128]{3,2,1,0:T(8,128)S(1)}, u32[]{:S(2)}, u32[]{:S(2)}) collective-permute-start(f32[8,2,64,128]{3,2,1,0:T(8,128)S(1)} %add.205), channel_id=1, source_target_pairs={{0,128},{16,144},{32,160},{48,176},{64,192},{80,208},{96,224},{112... | collective-permute-start | bytes 1572872 | tf_op jit(solution)/shard_map/ppermute | solution.py:23
  64.2 15.0 %collective-permute-start.4 = (f32[8,2,64,128]{3,2,1,0:T(8,128)S(1)}, f32[8,2,64,128]{3,2,1,0:T(8,128)S(1)}, u32[]{:S(2)}, u32[]{:S(2)}) collective-permute-start(f32[8,2,64,128]{3,2,1,0:T(8,128)S(1)} %add.206), channel_id=1, source_target_pairs={{0,256},{16,272},{32,288},{48,304},{64,320},{80,336},{96,352},{112... | collective-permute-start | bytes 1572872 | tf_op jit(solution)/shard_map/ppermute | solution.py:23
  80.0 40.0 %collective-permute-start.5 = (f32[64,128]{1,0:T(8,128)S(1)}, f32[64,128]{1,0:T(8,128)S(1)}, u32[]{:S(2)}, u32[]{:S(2)}) collective-permute-start(f32[64,128]{1,0:T(8,128)S(1)} %fusion.34), channel_id=1, source_target_pairs={{0,64},{16,80},{32,96},{48,112},{64,0},{80,16},{96,32},{112,48},{1... | collective-permute-start | bytes 98312 | tf_op jit(solution)/shard_map/ppermute | solution.py:12
  149.7 0.8 copy-start.5
  149.7 0.9 copy-start.8
  150.9 3.4 collective-permute-start.6
  154.4 10.2 %collective-permute-start.7 = (f32[4,2,64,128]{3,2,1,0:T(8,128)S(1)}, f32[4,2,64,128]{3,2,1,0:T(8,128)S(1)}, u32[]{:S(2)}, u32[]{:S(2)}) collective-permute-start(f32[4,2,64,128]{3,2,1,0:T(8,128)S(1)} %fusion.30), channel_id=1, source_target_pairs={{0,32},{16,48},{32,0},{48,16},{64,96},{80,112},{96,64},{112,80},{1... | collective-permute-start | bytes 786440 | tf_op jit(solution)/shard_map/ppermute | solution.py:23
  164.8 10.9 %collective-permute-start.8 = (f32[4,2,64,128]{3,2,1,0:T(8,128)S(1)}, f32[4,2,64,128]{3,2,1,0:T(8,128)S(1)}, u32[]{:S(2)}, u32[]{:S(2)}) collective-permute-start(f32[4,2,64,128]{3,2,1,0:T(8,128)S(1)} %fusion.89), channel_id=1, source_target_pairs={{0,64},{16,80},{32,96},{48,112},{64,0},{80,16},{96,32},{112,48},{1... | collective-permute-start | bytes 786440 | tf_op jit(solution)/shard_map/ppermute | solution.py:23
  175.7 8.5 collective-permute-start.9
  184.2 9.8 %collective-permute-start.10 = (f32[4,2,64,128]{3,2,1,0:T(8,128)S(1)}, f32[4,2,64,128]{3,2,1,0:T(8,128)S(1)}, u32[]{:S(2)}, u32[]{:S(2)}) collective-permute-start(f32[4,2,64,128]{3,2,1,0:T(8,128)S(1)} %add.219), channel_id=1, source_target_pairs={{0,256},{16,272},{32,288},{48,304},{64,320},{80,336},{96,352},{112... | collective-permute-start | bytes 786440 | tf_op jit(solution)/shard_map/ppermute | solution.py:23
  194.0 363.2 %copy-start.2 = (f32[1,2,64,128]{3,2,1,0:T(8,128)}, f32[1,2,64,128]{3,2,1,0:T(8,128)S(1)}, u32[]{:S(2)}) copy-start(f32[1,2,64,128]{3,2,1,0:T(8,128)S(1)} %dynamic-slice_add_fusion.1) | copy-start | bytes 196612
  194.1 34.8 %collective-permute-start.11 = (f32[64,128]{1,0:T(8,128)S(1)}, f32[64,128]{1,0:T(8,128)S(1)}, u32[]{:S(2)}, u32[]{:S(2)}) collective-permute-start(f32[64,128]{1,0:T(8,128)S(1)} %fusion.33), channel_id=1, source_target_pairs={{0,128},{16,144},{32,160},{48,176},{64,192},{80,208},{96,224},{112... | collective-permute-start | bytes 98312 | tf_op jit(solution)/shard_map/ppermute | solution.py:12
  258.6 0.8 copy-start.4
  258.6 0.8 copy-start.9
  259.7 3.2 collective-permute-start.12
  263.0 7.4 collective-permute-start.13
  270.6 8.4 collective-permute-start.14
  279.0 6.9 collective-permute-start.15
  285.8 8.4 collective-permute-start.16
  294.2 179.8 %copy-start.3 = (f32[1,2,64,128]{3,2,1,0:T(8,128)}, f32[1,2,64,128]{3,2,1,0:T(8,128)S(1)}, u32[]{:S(2)}) copy-start(f32[1,2,64,128]{3,2,1,0:T(8,128)S(1)} %dynamic-slice_add_fusion) | copy-start | bytes 196612
  294.2 36.6 %collective-permute-start.17 = (f32[64,128]{1,0:T(8,128)S(1)}, f32[64,128]{1,0:T(8,128)S(1)}, u32[]{:S(2)}, u32[]{:S(2)}) collective-permute-start(f32[64,128]{1,0:T(8,128)S(1)} %fusion.32), channel_id=1, source_target_pairs={{0,256},{16,272},{32,288},{48,304},{64,320},{80,336},{96,352},{112... | collective-permute-start | bytes 98312 | tf_op jit(solution)/shard_map/ppermute | solution.py:12
  360.8 0.8 copy-start.7
  361.0 27.1 %copy-start.1 = (f32[1024,128]{1,0:T(8,128)S(1)}, f32[1024,128]{1,0:T(8,128)}, u32[]{:S(2)}) copy-start(f32[1024,128]{1,0:T(8,128)} %param.20) | copy-start | bytes 1572868
  361.8 3.1 collective-permute-start.18
  365.0 6.2 collective-permute-start.19
  371.2 7.7 collective-permute-start.20
  378.8 6.2 collective-permute-start.21
  385.0 7.7 collective-permute-start.22
  447.5 3.1 collective-permute-start.23
  450.5 5.8 collective-permute-start.24
  456.4 7.7 collective-permute-start.25
  464.0 6.9 collective-permute-start.26
  470.9 9.8 %collective-permute-start.27 = (f32[512,128]{1,0:T(8,128)S(1)}, f32[512,128]{1,0:T(8,128)S(1)}, u32[]{:S(2)}, u32[]{:S(2)}) collective-permute-start(f32[512,128]{1,0:T(8,128)S(1)} %maximum_select_fusion.3), channel_id=1, source_target_pairs={{0,256},{16,272},{32,288},{48,304},{64,320},{80,336},{96,352},{112... | collective-permute-start | bytes 786440 | tf_op jit(solution)/shard_map/ppermute | solution.py:12
  481.9 0.8 slice-start.1
  535.7 3.1 collective-permute-start.28
  538.8 6.2 collective-permute-start.29
  544.9 8.4 collective-permute-start.30
  553.3 8.3 collective-permute-start.31
  564.6 281.6 %all-reduce.5.cloned.1.call-start = ((), (), s32[]{:S(2)}) async-start(), calls=%async_computation.1 | async-start | bytes 262144 | tf_op jit(solution)/shard_map/psum | solution.py:128
  690.6 3.3 collective-permute-start.32
  694.9 7.5 collective-permute-start.33
  702.4 10.9 %collective-permute-start.34 = (f32[512,128]{0,1:T(8,128)S(1)}, f32[512,128]{0,1:T(8,128)S(1)}, u32[]{:S(2)}, u32[]{:S(2)}) collective-permute-start(f32[512,128]{0,1:T(8,128)S(1)} %maximum_select_fusion.5), channel_id=1, source_target_pairs={{0,64},{16,80},{32,96},{48,112},{64,0},{80,16},{96,32},{112,48},{1... | collective-permute-start | bytes 786440 | tf_op jit(solution)/shard_map/ppermute | solution.py:12
  715.9 0.8 copy-start.6
  (2 other events, 1.5 us)
Sparse Core Ops, SparseCore 0:
  564.7 125.8 all-reduce.2
  716.1 130.0 all-reduce.4
